TPU v7x, 32 devices: a whole 2x2x4 slice. The times are simulated.
32 devices in a mesh: tm: 16 (over z, y, core), band: 2 (over x).
Axes of the slice: x: 2, y: 2, z: 4, core: 2. Of those that a mesh axis runs over, the one named last changes fastest.
Arguments:
- feats: bfloat16 [16, 16, 128, 256], P('tm', 'band'), may hold values from -6 to 6
- cotangent: bfloat16 [16, 16, 128, 256], P('tm', 'band'), may hold values from -6 to 6
- w_value: bfloat16 [256, 256], replicated, may hold values from -0.375 to 0.375
- w_logit: bfloat16 [256, 48], replicated, may hold values from -24 to 24
- w_out: bfloat16 [256, 256], replicated, may hold values from -0.375 to 0.375
- row_offsets: int32 [16, 5, 16, 128], P('tm', None, 'band'), may hold values from -1 to 0
- col_offsets: int32 [16, 5, 16, 128], P('tm', None, 'band'), may hold values from -8 to 7
- fractions: int32 [16, 2, 5, 16, 128], P('tm', None, None, 'band'), may hold values from 0 to 7
- present: int32 [16, 5], P('tm'), may hold values 0 or 1
Outputs:
- grad_feats: bfloat16 [16, 16, 128, 256], P('tm', 'band')
- grad_w_value: float32 [256, 256], replicated
- grad_w_logit: float32 [256, 48], replicated
- grad_w_out: float32 [256, 256], replicated
All inputs are finite; a program needn't handle non-finite values. No bound on the sum of `present` on one device may be relied on, other than what follows from the above.
Results may differ from a plain program's by a relative error of at most 0.014.
Values may be sent and summed in bfloat16 or wider, within the bound.
A program may use at most 64 MiB of HBM per device.

v0:
```python
import jax
import jax.numpy as jnp
from jax import lax
from jax.sharding import PartitionSpec as P

H = 8
E = 32
K = 5
J = 6
REACH = 1


DISTANCES = (1, 2, 4, 8, 16)


def extended_2(block, sides, width):
    for axis, dim in sides:
        count = lax.axis_size(axis)
        forward = [(i, i + 1) for i in range(count - 1)]
        backward = [(target, source) for source, target in forward]
        low = lax.ppermute(
            lax.slice_in_dim(block, block.shape[dim] - width, None, axis=dim), axis, forward
        )
        high = lax.ppermute(lax.slice_in_dim(block, 0, width, axis=dim), axis, backward)
        block = jnp.concatenate([low, block, high], axis=dim)
    return block


def shifted(value, axis, steps):
    count = lax.axis_size(axis)
    initial, last = (max(0, -steps), min(count, count - steps))
    return lax.ppermute(value, axis, [(source, source + steps) for source in range(initial, last)])


def corner_table(row_shift, col_shift, row_frac, col_frac, row_count, column_count, reach_rows):
    queries = row_count * column_count
    cell_index = jnp.arange(queries, dtype=jnp.int32)
    row_here = cell_index // column_count
    col_here = cell_index % column_count
    source = jnp.arange((row_count + 2 * reach_rows) * column_count, dtype=jnp.int32)
    table = jnp.zeros((queries, source.shape[0]), jnp.float32)
    for row_step in (0, 1):
        if row_step == 0:
            row_weight = 8 - row_frac
        else:
            row_weight = row_frac
        for col_step in (0, 1):
            if col_step == 0:
                col_weight = 8 - col_frac
            else:
                col_weight = col_frac
            ext_row = row_here + row_shift + row_step + reach_rows
            ext_col = col_here + col_shift + col_step
            inside = (ext_col >= 0) & (ext_col < column_count)
            target = ext_row * column_count + ext_col
            weight = jnp.where(
                inside, (row_weight * col_weight).astype(jnp.float32) / 64.0, jnp.float32(0.0)
            )
            table = table + jnp.where(
                source[None, :] == target[:, None], weight[:, None], jnp.float32(0.0)
            )
    return table.astype(jnp.bfloat16)


def transposed_product(table, operand):
    return lax.dot_general(
        table, operand, (((0,), (0,)), ((), ())), preferred_element_type=jnp.float32
    )


def shards(feats, cotangent, w_value, w_logit, w_out, row_offsets, col_offsets, fractions, present):
    row_count = feats.shape[1]
    column_count = feats.shape[2]
    channels = feats.shape[3]
    queries = row_count * column_count
    inputs = feats.reshape(queries, channels)
    grad_out = cotangent.reshape(queries, channels)
    frame_index = lax.axis_index("tm")
    values = jnp.dot(inputs, w_value, preferred_element_type=jnp.float32).astype(jnp.bfloat16)
    value_grid = values.reshape(row_count, column_count, channels)
    extended = extended_2(value_grid, (("band", 0),), REACH)
    extended = extended.reshape((row_count + 2 * REACH) * column_count, channels)
    row_shift = row_offsets.reshape(K, queries)
    col_shift = col_offsets.reshape(K, queries)
    frac_rows = fractions[0, 0].reshape(K, queries)
    frac_cols = fractions[0, 1].reshape(K, queries)
    tables = []
    sampled = [values]
    for slot in range(K):
        distance = DISTANCES[slot]
        packed = jnp.stack([row_shift[slot], col_shift[slot], frac_rows[slot], frac_cols[slot]])
        arrived = shifted(packed, "tm", -distance)
        table = corner_table(
            arrived[0], arrived[1], arrived[2], arrived[3], row_count, column_count, REACH
        )
        local_sample = jnp.dot(table, extended, preferred_element_type=jnp.float32).astype(
            jnp.bfloat16
        )
        taken = shifted(local_sample, "tm", distance)
        tables.append(table)
        sampled.append(taken)
    valid = [jnp.asarray(True)]
    for slot in range(K):
        valid.append((present[0, slot] == 1) & (frame_index >= DISTANCES[slot]))
    valid_vec = jnp.stack(valid)
    logits = jnp.dot(inputs, w_logit, preferred_element_type=jnp.float32).reshape(queries, H, J)
    masked = jnp.where(valid_vec[None, None, :], logits, jnp.float32(-1e30))
    top = jnp.max(masked, axis=2, keepdims=True)
    expo = jnp.where(valid_vec[None, None, :], jnp.exp(masked - top), jnp.float32(0.0))
    attn = expo / jnp.sum(expo, axis=2, keepdims=True)
    attn_low = attn.astype(jnp.bfloat16)
    stacked = jnp.stack(sampled).reshape(J, queries, H, E)
    mixed = jnp.einsum("qhj,jqhe->qhe", attn_low, stacked, preferred_element_type=jnp.float32)
    mixed = mixed.reshape(queries, channels).astype(jnp.bfloat16)
    d_mixed = jnp.dot(grad_out, w_out.T, preferred_element_type=jnp.float32).astype(jnp.bfloat16)
    d_heads = d_mixed.reshape(queries, H, E)
    d_attn = jnp.einsum("qhe,jqhe->qhj", d_heads, stacked, preferred_element_type=jnp.float32)
    d_logits = attn * (d_attn - jnp.sum(attn * d_attn, axis=2, keepdims=True))
    d_logit_low = d_logits.reshape(queries, H * J).astype(jnp.bfloat16)
    d_sampled = jnp.einsum(
        "qhj,qhe->jqhe", attn_low, d_heads, preferred_element_type=jnp.float32
    ).astype(jnp.bfloat16)
    d_sampled = d_sampled.reshape(J, queries, channels)
    accum = jnp.zeros(((row_count + 2 * REACH) * column_count, channels), jnp.float32)
    for slot in range(K):
        distance = DISTANCES[slot]
        arrived_grad = shifted(d_sampled[slot + 1], "tm", -distance)
        accum = accum + transposed_product(tables[slot], arrived_grad)
    edge = REACH * column_count
    lower_rim = accum[:edge]
    upper_rim = accum[accum.shape[0] - edge :]
    center = accum[edge : edge + queries] + d_sampled[0].astype(jnp.float32)
    from_next = shifted(lower_rim.astype(jnp.bfloat16), "band", -1).astype(lower_rim.dtype)
    from_prev = shifted(upper_rim.astype(jnp.bfloat16), "band", 1).astype(upper_rim.dtype)
    center = center.at[:edge].add(from_prev)
    center = center.at[queries - edge :].add(from_next)
    d_value_low = center.astype(jnp.bfloat16)
    local_out = transposed_product(mixed, grad_out)
    local_value = transposed_product(inputs, d_value_low)
    local_logit = transposed_product(inputs, d_logit_low)
    summed = lax.psum((local_value, local_logit, local_out), ("tm", "band"))
    grad_in = grad_out.astype(jnp.float32) + jnp.dot(
        d_value_low, w_value.T, preferred_element_type=jnp.float32
    )
    grad_in = grad_in + jnp.dot(d_logit_low, w_logit.T, preferred_element_type=jnp.float32)
    grad_feats = grad_in.astype(jnp.bfloat16).reshape(feats.shape)
    return (grad_feats, summed[0], summed[1], summed[2])


def solution(mesh):
    placed = (
        P("tm", "band", None, None),
        P("tm", "band", None, None),
        P(),
        P(),
        P(),
        P("tm", None, "band", None),
        P("tm", None, "band", None),
        P("tm", None, None, "band", None),
        P("tm", None),
    )
    return jax.shard_map(
        shards,
        mesh=mesh,
        in_specs=placed,
        out_specs=(P("tm", "band", None, None), P(), P(), P()),
        check_vma=False,
    )
```

profile of v0, /device:TPU:0, one launch (start us, length us, event | category | flops | bytes accessed | tf_op | source)
XLA Modules:
  0.0 380.8 jit_solution(9449171657118764827)
XLA Ops:
  24.3 4.8 %collective-permute-start.12 = (bf16[1,128,256]{2,1,0:T(8,128)(2,1)S(1)}, bf16[1,128,256]{2,1,0:T(8,128)(2,1)S(1)}, u32[]{:S(2)}, u32[]{:S(2)}) collective-permute-start(bf16[1,128,256]{2,1,0:T(8,128)(2,1)S(1)} %get-tuple-element.68), channel_id=1, source_target_pairs={{0,1},{2,3},{4,5},{6,7},{8,9},{10,11},{12,13},{14,15},{16,17},{18,... | collective-permute-start | bytes 196616 | tf_op jit(solution)/shard_map/ppermute | solution.py:21
  31.5 4.6 %collective-permute-done.13 = bf16[1,128,256]{2,1,0:T(8,128)(2,1)S(1)} collective-permute-done((bf16[1,128,256]{2,1,0:T(8,128)(2,1)S(1)}, bf16[1,128,256]{2,1,0:T(8,128)(2,1)S(1)}, u32[]{:S(2)}, u32[]{:S(2)}) %collective-permute-start.13) | collective-permute-done | bytes 65568 | tf_op jit(solution)/shard_map/ppermute | solution.py:24
  36.2 3.5 convolution_convert_fusion.4
  41.7 4.1 %convolution_convert_fusion.3 = bf16[1024,256]{1,0:T(8,128)(2,1)} fusion(bf16[1280,256]{1,0:T(8,128)(2,1)S(1)} %bitcast.130, f32[1024]{0:T(1024)S(1)} %get-tuple-element.131, s32[1024]{0:T(1024)S(1)} %get-tuple-element.129, f32[1024]{0:T(1024)S(1)} %get-tuple-element.130, s32[1024]{0:T(1024)S(1)} %get-tuple-element.127, f32[1024]{0:T(1024)S(1)} %get-tuple-element.112, ...), kind=kOutput, calls=%fused_computation.39 | convolution fusion | flops 687079424 | bytes 1212416 | tf_op jit(solution)/shard_map/dot_general | solution.py:96
  45.8 5.4 %collective-permute-start.15 = (bf16[1024,256]{1,0:T(8,128)(2,1)}, bf16[1024,256]{1,0:T(8,128)(2,1)}, u32[]{:S(2)}, u32[]{:S(2)}) collective-permute-start(bf16[1024,256]{1,0:T(8,128)(2,1)} %convolution_convert_fusion.3), channel_id=1, source_target_pairs={{0,4},{2,6},{4,8},{6,10},{8,12},{10,14},{12,16},{14,18},{16,20},{1... | collective-permute-start | bytes 1572872 | tf_op jit(solution)/shard_map/ppermute | solution.py:32
  51.3 4.1 %convolution_convert_fusion.2 = bf16[1024,256]{1,0:T(8,128)(2,1)} fusion(bf16[1280,256]{1,0:T(8,128)(2,1)S(1)} %bitcast.131, f32[1024]{0:T(1024)S(1)} %get-tuple-element.137, s32[1024]{0:T(1024)S(1)} %get-tuple-element.135, f32[1024]{0:T(1024)S(1)} %get-tuple-element.136, s32[1024]{0:T(1024)S(1)} %get-tuple-element.133, f32[1024]{0:T(1024)S(1)} %get-tuple-element.114, ...), kind=kOutput, calls=%fused_computation.38 | convolution fusion | flops 687079424 | bytes 1212416 | tf_op jit(solution)/shard_map/dot_general | solution.py:96
  55.4 4.8 %collective-permute-start.16 = (bf16[1024,256]{1,0:T(8,128)(2,1)}, bf16[1024,256]{1,0:T(8,128)(2,1)}, u32[]{:S(2)}, u32[]{:S(2)}) collective-permute-start(bf16[1024,256]{1,0:T(8,128)(2,1)} %convolution_convert_fusion.2), channel_id=1, source_target_pairs={{0,8},{2,10},{4,12},{6,14},{8,16},{10,18},{12,20},{14,22},{16,24},... | collective-permute-start | bytes 1572872 | tf_op jit(solution)/shard_map/ppermute | solution.py:32
  60.2 4.1 %convolution_convert_fusion.1 = bf16[1024,256]{1,0:T(8,128)(2,1)} fusion(bf16[1280,256]{1,0:T(8,128)(2,1)S(1)} %bitcast.132, f32[1024]{0:T(1024)S(1)} %get-tuple-element.143, s32[1024]{0:T(1024)S(1)} %get-tuple-element.141, f32[1024]{0:T(1024)S(1)} %get-tuple-element.142, s32[1024]{0:T(1024)S(1)} %get-tuple-element.139, f32[1024]{0:T(1024)S(1)} %get-tuple-element.116, ...), kind=kOutput, calls=%fused_computation.37 | convolution fusion | flops 687079424 | bytes 1212416 | tf_op jit(solution)/shard_map/dot_general | solution.py:96
  64.3 5.3 %collective-permute-start.17 = (bf16[1024,256]{1,0:T(8,128)(2,1)}, bf16[1024,256]{1,0:T(8,128)(2,1)}, u32[]{:S(2)}, u32[]{:S(2)}) collective-permute-start(bf16[1024,256]{1,0:T(8,128)(2,1)} %convolution_convert_fusion.1), channel_id=1, source_target_pairs={{0,16},{2,18},{4,20},{6,22},{8,24},{10,26},{12,28},{14,30},{1,17},... | collective-permute-start | bytes 1572872 | tf_op jit(solution)/shard_map/ppermute | solution.py:32
  69.7 4.1 %convolution_convert_fusion = bf16[1024,256]{1,0:T(8,128)(2,1)} fusion(bf16[1280,256]{1,0:T(8,128)(2,1)S(1)} %bitcast.133, f32[1024]{0:T(1024)S(1)} %get-tuple-element.149, s32[1024]{0:T(1024)S(1)} %get-tuple-element.147, f32[1024]{0:T(1024)S(1)} %get-tuple-element.148, s32[1024]{0:T(1024)S(1)} %get-tuple-element.145, f32[1024]{0:T(1024)S(1)} %get-tuple-element.118, ...), kind=kOutput, calls=%fused_computation.36 | convolution fusion | flops 687079424 | bytes 1212416 | tf_op jit(solution)/shard_map/dot_general | solution.py:96
  79.6 2.4 collective-permute-done.17
  90.6 3.6 multiply_reduce_fusion.1
  96.3 56.9 %psum.22 = f32[256,48]{0,1:T(8,128)} all-reduce(f32[256,48]{0,1:T(8,128)S(1)} %convolution_bitcast_fusion.1), channel_id=1, replica_groups=mesh['tm'=16,'band'=2] {'tm','band'}, use_global_device_ids=true, to_apply=%region_4.5 | all-reduce | flops 12288 | bytes 98304 | tf_op jit(solution)/shard_map/psum | solution.py:141
  160.5 2.7 multiply_reduce_fusion
  164.3 11.9 %collective-permute-done.3 = bf16[1024,256]{0,1:T(8,128)(2,1)} collective-permute-done((bf16[1024,256]{0,1:T(8,128)(2,1)}, bf16[1024,256]{0,1:T(8,128)(2,1)}, u32[]{:S(2)}, u32[]{:S(2)}) %collective-permute-start.3) | collective-permute-done | bytes 524320 | tf_op jit(solution)/shard_map/ppermute | solution.py:32
  176.3 4.2 %fusion.5 = f32[1280,256]{1,0:T(8,128)S(1)} fusion(bf16[1024,256]{0,1:T(8,128)(2,1)} %collective-permute-done.3, f32[1024]{0:T(1024)S(1)} %copy-done.36, s32[1024]{0:T(1024)S(1)} %copy-done.28, f32[1024]{0:T(1024)S(1)} %copy-done.34, s32[1024]{0:T(1024)S(1)} %copy-done.24, f32[1024]{0:T(1024)S(1)} %copy-done.32, s32[1024]{0:T(1024)S(1)} %copy-done.26, ...), kind=kOutput, calls=%fused_computation.45 | convolution fusion | flops 686817280 | bytes 1867776 | tf_op jit(solution)/shard_map/dot_general | solution.py:66
  180.5 5.7 %collective-permute-done.5 = bf16[1024,256]{0,1:T(8,128)(2,1)} collective-permute-done((bf16[1024,256]{0,1:T(8,128)(2,1)}, bf16[1024,256]{0,1:T(8,128)(2,1)}, u32[]{:S(2)}, u32[]{:S(2)}) %collective-permute-start.5) | collective-permute-done | bytes 524320 | tf_op jit(solution)/shard_map/ppermute | solution.py:32
  186.3 4.2 %fusion.6 = f32[1280,256]{1,0:T(8,128)S(1)} fusion(bf16[1024,256]{0,1:T(8,128)(2,1)} %collective-permute-done.5, f32[1024]{0:T(1024)S(1)} %copy-done.52, s32[1024]{0:T(1024)S(1)} %copy-done.44, f32[1024]{0:T(1024)S(1)} %copy-done.50, s32[1024]{0:T(1024)S(1)} %copy-done.40, f32[1024]{0:T(1024)S(1)} %copy-done.48, s32[1024]{0:T(1024)S(1)} %copy-done.42, ...), kind=kOutput, calls=%fused_computation.46 | convolution fusion | flops 686817280 | bytes 1867776 | tf_op jit(solution)/shard_map/dot_general | solution.py:66
  190.5 3.0 collective-permute-done.7
  193.5 4.2 %fusion.7 = f32[1280,256]{1,0:T(8,128)S(1)} fusion(bf16[1024,256]{0,1:T(8,128)(2,1)} %collective-permute-done.7, f32[1024]{0:T(1024)S(1)} %copy-done.80, s32[1024]{0:T(1024)S(1)} %copy-done.60, f32[1024]{0:T(1024)S(1)} %copy-done.78, s32[1024]{0:T(1024)S(1)} %copy-done.56, f32[1024]{0:T(1024)S(1)} %copy-done.72, s32[1024]{0:T(1024)S(1)} %copy-done.58, ...), kind=kOutput, calls=%fused_computation.47 | convolution fusion | flops 686817280 | bytes 1867776 | tf_op jit(solution)/shard_map/dot_general | solution.py:66
  197.8 4.4 %fusion.8 = f32[1280,256]{1,0:T(8,128)S(1)} fusion(bf16[1024,256]{0,1:T(8,128)(2,1)} %collective-permute-done.9, f32[1024]{0:T(1024)S(1)} %copy-done.20, s32[1024]{0:T(1024)S(1)} %copy-done.12, f32[1024]{0:T(1024)S(1)} %copy-done.18, s32[1024]{0:T(1024)S(1)} %get-tuple-element.145, f32[1024]{0:T(1024)S(1)} %copy-done.16, s32[1024]{0:T(1024)S(1)} %get-tuple-element.146, ...), kind=kOutput, calls=%fused_computation.48 | convolution fusion | flops 686817280 | bytes 1867776 | tf_op jit(solution)/shard_map/dot_general | solution.py:66
  202.3 4.4 %fusion.75 = (bf16[1280,256]{1,0:T(8,128)(2,1)S(1)}, f32[1280,256]{1,0:T(8,128)S(1)}) fusion(f32[1280,256]{1,0:T(8,128)S(1)} %fusion.8, f32[1280,256]{1,0:T(8,128)S(1)} %fusion.7, f32[1280,256]{1,0:T(8,128)S(1)} %fusion.6, f32[1280,256]{1,0:T(8,128)S(1)} %fusion.5, bf16[1024,256]{0,1:T(8,128)(2,1)} %collective-permute-done.1, f32[1024]{0:T(1024)S(1)} %copy-done.84, ...), kind=kOutput, calls=%fused_computation.183 | convolution fusion | flops 688455680 | bytes 7766016 | tf_op jit(solution)/shard_map/dot_general | solution.py:66
  208.2 4.5 %collective-permute-start.10 = (bf16[128,256]{1,0:T(8,128)(2,1)S(1)}, bf16[128,256]{1,0:T(8,128)(2,1)S(1)}, u32[]{:S(2)}, u32[]{:S(2)}) collective-permute-start(bf16[128,256]{1,0:T(8,128)(2,1)S(1)} %get-tuple-element.67), channel_id=1, source_target_pairs={{0,1},{2,3},{4,5},{6,7},{8,9},{10,11},{12,13},{14,15},{16,17},{18,... | collective-permute-start | bytes 196616 | tf_op jit(solution)/shard_map/ppermute | solution.py:32
  217.2 153.2 %all-reduce.3.cloned.1.call-done = (f32[256,256]{0,1:T(8,128)}, f32[256,256]{1,0:T(8,128)}) async-done(((f32[256,256]{0,1:T(8,128)}, f32[256,256]{1,0:T(8,128)}), (f32[256,256]{0,1:T(8,128)}, f32[256,256]{1,0:T(8,128)})) %all-reduce.3.cloned.1.call-update) | async-done | bytes 524304 | tf_op jit(solution)/shard_map/psum | solution.py:141
  (268 shorter events, 51.8 us)
Async XLA Ops:
  7.2 363.3 %all-reduce.3.cloned.1.call-start = ((), (), s32[]{:S(2)}) async-start(), calls=%async_computation | async-start | bytes 1048576 | tf_op jit(solution)/shard_map/psum | solution.py:141
  9.7 14.7 %collective-permute-start.8 = (s32[4,1024]{1,0:T(4,128)S(1)}, s32[4,1024]{1,0:T(4,128)S(1)}, u32[]{:S(2)}, u32[]{:S(2)}) collective-permute-start(s32[4,1024]{1,0:T(4,128)S(1)} %pad_add_fusion.4), channel_id=1, source_target_pairs={} | collective-permute-start | bytes 49160 | tf_op jit(solution)/shard_map/ppermute | solution.py:32
  10.4 18.9 %collective-permute-start.2 = (s32[4,1024]{1,0:T(4,128)S(1)}, s32[4,1024]{1,0:T(4,128)S(1)}, u32[]{:S(2)}, u32[]{:S(2)}) collective-permute-start(s32[4,1024]{1,0:T(4,128)S(1)} %pad_add_fusion.1), channel_id=1, source_target_pairs={{4,0},{6,2},{8,4},{10,6},{12,8},{14,10},{16,12},{18,14},{20,16},{2... | collective-permute-start | bytes 49160 | tf_op jit(solution)/shard_map/ppermute | solution.py:32
  11.7 19.1 %collective-permute-start.4 = (s32[4,1024]{1,0:T(4,128)S(1)}, s32[4,1024]{1,0:T(4,128)S(1)}, u32[]{:S(2)}, u32[]{:S(2)}) collective-permute-start(s32[4,1024]{1,0:T(4,128)S(1)} %pad_add_fusion.2), channel_id=1, source_target_pairs={{8,0},{10,2},{12,4},{14,6},{16,8},{18,10},{20,12},{22,14},{24,16},... | collective-permute-start | bytes 49160 | tf_op jit(solution)/shard_map/ppermute | solution.py:32
  13.0 17.9 %collective-permute-start.6 = (s32[4,1024]{1,0:T(4,128)S(1)}, s32[4,1024]{1,0:T(4,128)S(1)}, u32[]{:S(2)}, u32[]{:S(2)}) collective-permute-start(s32[4,1024]{1,0:T(4,128)S(1)} %pad_add_fusion.3), channel_id=1, source_target_pairs={{16,0},{18,2},{20,4},{22,6},{24,8},{26,10},{28,12},{30,14},{17,1},... | collective-permute-start | bytes 49160 | tf_op jit(solution)/shard_map/ppermute | solution.py:32
  14.4 16.7 %collective-permute-start = (s32[4,1024]{1,0:T(4,128)S(1)}, s32[4,1024]{1,0:T(4,128)S(1)}, u32[]{:S(2)}, u32[]{:S(2)}) collective-permute-start(s32[4,1024]{1,0:T(4,128)S(1)} %pad_add_fusion), channel_id=1, source_target_pairs={{2,0},{4,2},{6,4},{8,6},{10,8},{12,10},{14,12},{16,14},{18,16},{20... | collective-permute-start | bytes 49160 | tf_op jit(solution)/shard_map/ppermute | solution.py:32
  24.3 7.1 %collective-permute-start.12 = (bf16[1,128,256]{2,1,0:T(8,128)(2,1)S(1)}, bf16[1,128,256]{2,1,0:T(8,128)(2,1)S(1)}, u32[]{:S(2)}, u32[]{:S(2)}) collective-permute-start(bf16[1,128,256]{2,1,0:T(8,128)(2,1)S(1)} %get-tuple-element.68), channel_id=1, source_target_pairs={{0,1},{2,3},{4,5},{6,7},{8,9},{10,11},{12,13},{14,15},{16,17},{18,... | collective-permute-start | bytes 196616 | tf_op jit(solution)/shard_map/ppermute | solution.py:21
  29.2 40.4 %copy-start.11 = (s32[1024]{0:T(1024)}, s32[1024]{0:T(1024)S(1)}, u32[]{:S(2)}) copy-start(s32[1024]{0:T(1024)S(1)} %get-tuple-element.147) | copy-start | bytes 12292
  29.2 40.4 %copy-start.13 = (f32[1024]{0:T(1024)}, f32[1024]{0:T(1024)S(1)}, u32[]{:S(2)}) copy-start(f32[1024]{0:T(1024)S(1)} %get-tuple-element.54) | copy-start | bytes 12292
  29.3 40.4 %copy-start.15 = (f32[1024]{0:T(1024)}, f32[1024]{0:T(1024)S(1)}, u32[]{:S(2)}) copy-start(f32[1024]{0:T(1024)S(1)} %get-tuple-element.118) | copy-start | bytes 12292
  29.3 40.4 %copy-start.17 = (f32[1024]{0:T(1024)}, f32[1024]{0:T(1024)S(1)}, u32[]{:S(2)}) copy-start(f32[1024]{0:T(1024)S(1)} %get-tuple-element.148) | copy-start | bytes 12292
  29.3 6.7 %collective-permute-start.13 = (bf16[1,128,256]{2,1,0:T(8,128)(2,1)S(1)}, bf16[1,128,256]{2,1,0:T(8,128)(2,1)S(1)}, u32[]{:S(2)}, u32[]{:S(2)}) collective-permute-start(bf16[1,128,256]{2,1,0:T(8,128)(2,1)S(1)} %get-tuple-element.69), channel_id=1, source_target_pairs={{1,0},{3,2},{5,4},{7,6},{9,8},{11,10},{13,12},{15,14},{17,16},{19,... | collective-permute-start | bytes 196616 | tf_op jit(solution)/shard_map/ppermute | solution.py:24
  39.7 36.4 %collective-permute-start.14 = (bf16[1024,256]{1,0:T(8,128)(2,1)S(1)}, bf16[1024,256]{1,0:T(8,128)(2,1)S(1)}, u32[]{:S(2)}, u32[]{:S(2)}) collective-permute-start(bf16[1024,256]{1,0:T(8,128)(2,1)S(1)} %convolution_convert_fusion.4), channel_id=1, source_target_pairs={{0,2},{2,4},{4,6},{6,8},{8,10},{10,12},{12,14},{14,16},{16,18},{18... | collective-permute-start | bytes 1572872 | tf_op jit(solution)/shard_map/ppermute | solution.py:32
  45.8 30.5 %collective-permute-start.15 = (bf16[1024,256]{1,0:T(8,128)(2,1)}, bf16[1024,256]{1,0:T(8,128)(2,1)}, u32[]{:S(2)}, u32[]{:S(2)}) collective-permute-start(bf16[1024,256]{1,0:T(8,128)(2,1)} %convolution_convert_fusion.3), channel_id=1, source_target_pairs={{0,4},{2,6},{4,8},{6,10},{8,12},{10,14},{12,16},{14,18},{16,20},{1... | collective-permute-start | bytes 1572872 | tf_op jit(solution)/shard_map/ppermute | solution.py:32
  55.4 22.2 %collective-permute-start.16 = (bf16[1024,256]{1,0:T(8,128)(2,1)}, bf16[1024,256]{1,0:T(8,128)(2,1)}, u32[]{:S(2)}, u32[]{:S(2)}) collective-permute-start(bf16[1024,256]{1,0:T(8,128)(2,1)} %convolution_convert_fusion.2), channel_id=1, source_target_pairs={{0,8},{2,10},{4,12},{6,14},{8,16},{10,18},{12,20},{14,22},{16,24},... | collective-permute-start | bytes 1572872 | tf_op jit(solution)/shard_map/ppermute | solution.py:32
  64.3 17.7 %collective-permute-start.17 = (bf16[1024,256]{1,0:T(8,128)(2,1)}, bf16[1024,256]{1,0:T(8,128)(2,1)}, u32[]{:S(2)}, u32[]{:S(2)}) collective-permute-start(bf16[1024,256]{1,0:T(8,128)(2,1)} %convolution_convert_fusion.1), channel_id=1, source_target_pairs={{0,16},{2,18},{4,20},{6,22},{8,24},{10,26},{12,28},{14,30},{1,17},... | collective-permute-start | bytes 1572872 | tf_op jit(solution)/shard_map/ppermute | solution.py:32
  73.8 14.7 %collective-permute-start.18 = (bf16[1024,256]{1,0:T(8,128)(2,1)}, bf16[1024,256]{1,0:T(8,128)(2,1)}, u32[]{:S(2)}, u32[]{:S(2)}) collective-permute-start(bf16[1024,256]{1,0:T(8,128)(2,1)} %convolution_convert_fusion), channel_id=1, source_target_pairs={} | collective-permute-start | bytes 1572872 | tf_op jit(solution)/shard_map/ppermute | solution.py:32
  153.2 49.1 %collective-permute-start.1 = (bf16[1024,256]{0,1:T(8,128)(2,1)}, bf16[1024,256]{0,1:T(8,128)(2,1)}, u32[]{:S(2)}, u32[]{:S(2)}) collective-permute-start(bf16[1024,256]{0,1:T(8,128)(2,1)} %bitcast.26), channel_id=1, source_target_pairs={{2,0},{4,2},{6,4},{8,6},{10,8},{12,10},{14,12},{16,14},{18,16},{20... | collective-permute-start | bytes 1572872 | tf_op jit(solution)/shard_map/ppermute | solution.py:32
  154.4 43.3 %collective-permute-start.9 = (bf16[1024,256]{0,1:T(8,128)(2,1)}, bf16[1024,256]{0,1:T(8,128)(2,1)}, u32[]{:S(2)}, u32[]{:S(2)}) collective-permute-start(bf16[1024,256]{0,1:T(8,128)(2,1)} %bitcast.62), channel_id=1, source_target_pairs={} | collective-permute-start | bytes 1572872 | tf_op jit(solution)/shard_map/ppermute | solution.py:32
  155.9 37.6 %collective-permute-start.7 = (bf16[1024,256]{0,1:T(8,128)(2,1)}, bf16[1024,256]{0,1:T(8,128)(2,1)}, u32[]{:S(2)}, u32[]{:S(2)}) collective-permute-start(bf16[1024,256]{0,1:T(8,128)(2,1)} %bitcast.53), channel_id=1, source_target_pairs={{16,0},{18,2},{20,4},{22,6},{24,8},{26,10},{28,12},{30,14},{17,1},... | collective-permute-start | bytes 1572872 | tf_op jit(solution)/shard_map/ppermute | solution.py:32
  157.2 29.0 %collective-permute-start.5 = (bf16[1024,256]{0,1:T(8,128)(2,1)}, bf16[1024,256]{0,1:T(8,128)(2,1)}, u32[]{:S(2)}, u32[]{:S(2)}) collective-permute-start(bf16[1024,256]{0,1:T(8,128)(2,1)} %bitcast.44), channel_id=1, source_target_pairs={{8,0},{10,2},{12,4},{14,6},{16,8},{18,10},{20,12},{22,14},{24,16},... | collective-permute-start | bytes 1572872 | tf_op jit(solution)/shard_map/ppermute | solution.py:32
  158.5 17.7 %collective-permute-start.3 = (bf16[1024,256]{0,1:T(8,128)(2,1)}, bf16[1024,256]{0,1:T(8,128)(2,1)}, u32[]{:S(2)}, u32[]{:S(2)}) collective-permute-start(bf16[1024,256]{0,1:T(8,128)(2,1)} %bitcast.35), channel_id=1, source_target_pairs={{4,0},{6,2},{8,4},{10,6},{12,8},{14,10},{16,12},{18,14},{20,16},{2... | collective-permute-start | bytes 1572872 | tf_op jit(solution)/shard_map/ppermute | solution.py:32
  206.8 7.9 %collective-permute-start.11 = (bf16[128,256]{1,0:T(8,128)(2,1)S(1)}, bf16[128,256]{1,0:T(8,128)(2,1)S(1)}, u32[]{:S(2)}, u32[]{:S(2)}) collective-permute-start(bf16[128,256]{1,0:T(8,128)(2,1)S(1)} %get-tuple-element.66), channel_id=1, source_target_pairs={{1,0},{3,2},{5,4},{7,6},{9,8},{11,10},{13,12},{15,14},{17,16},{19,... | collective-permute-start | bytes 196616 | tf_op jit(solution)/shard_map/ppermute | solution.py:32
  208.2 6.4 %collective-permute-start.10 = (bf16[128,256]{1,0:T(8,128)(2,1)S(1)}, bf16[128,256]{1,0:T(8,128)(2,1)S(1)}, u32[]{:S(2)}, u32[]{:S(2)}) collective-permute-start(bf16[128,256]{1,0:T(8,128)(2,1)S(1)} %get-tuple-element.67), channel_id=1, source_target_pairs={{0,1},{2,3},{4,5},{6,7},{8,9},{10,11},{12,13},{14,15},{16,17},{18,... | collective-permute-start | bytes 196616 | tf_op jit(solution)/shard_map/ppermute | solution.py:32
  (81 other events, 1135.7 us)
Sparse Core Ops, SparseCore 0:
  216.2 154.1 all-reduce.2
where the time goes:
time: 382 us; the launch traced here: 381 us
  waiting for transfers between devices  183 us (48%)
  blocking collectives  56.9 us (15%)
  matrix products  46.7 us (12%)
  starting transfers between devices  43.5 us (11%)
  local copies, waits for them, and re-layouts  24.5 us (6%)
  between operations  19 us (5%)
  other arithmetic  7.31 us (2%)
    psum x1, waiting for transfers between devices, shards(): summed = lax.psum((local_value, local_logit, local_out), ('tm', 'band'))  153 us
    psum x1, blocking collectives, shards(): summed = lax.psum((local_value, local_logit, local_out), ('tm', 'band'))  56.9 us
    ppermute x17, starting transfers between devices, shifted(): lax.ppermute(value, axis, [(source, source + steps) for source in range(i...  37.4 us
    ppermute x17, waiting for transfers between devices, shifted(): lax.ppermute(value, axis, [(source, source + steps) for source in range(i...  24.7 us
    dot_general x8, matrix products, transposed_product(): lax.dot_general(table, operand, (((0,), (0,)), ((), ())), preferred_eleme...  23.5 us
    dot_general x5, matrix products, shards(): jnp.dot(table, extended, preferred_element_type=jnp.float32)  20 us
    unnamed x177, local copies, waits for them, and re-layouts  9.09 us
  transfers between devices with their start and end apart: 20, of which 8 were waited for; matrix products, arithmetic and copies ran while one was open for 15% of the time, Pallas kernels for 0%

commit v1 on v0

v1 whole, which is shorter than its diff:
```python
import functools

import jax
import jax.numpy as jnp
from jax import lax
from jax.experimental import pallas as pl
from jax.experimental.pallas import tpu as pltpu
from jax.sharding import PartitionSpec as P

H = 8
E = 32
K = 5
J = 6
DISTANCES = (1, 2, 4, 8, 16)
CHUNK = 16
MESH = pl.DeviceIdType.MESH
F32 = jnp.float32
BF16 = jnp.bfloat16


def nt_dot(a, b):
    return lax.dot_general(a, b, (((1,), (1,)), ((), ())), preferred_element_type=F32)


def dot(a, b):
    return jnp.dot(a, b, preferred_element_type=F32)


def spread_heads(a):
    return jnp.concatenate([jnp.broadcast_to(a[h : h + 1], (E, a.shape[1])) for h in range(H)], axis=0)


def head_sums(x):
    return jnp.sum(x.reshape(H, E, x.shape[1]), axis=1)


def kernel(
    nt, nb, owners,
    feats, cot, w_value, w_value_t, w_out, wl_t, wl, row_off, col_off, frac, present,
    out_feats, out_value, out_logit, out_wout,
    val, ext, tables, attn, dmix, dattn, mix, dlog, acc, cout, cin, rim_out, rim_in,
    g_out, g_val, g_log, s_out, s_val, s_log, r_out, r_val, r_log,
    band_part, whole, gathered,
    fs, fr, hs, hr, bs, br, ms, mr, ros, ror, rvs, rvr, rls, rlr, xs, xr, gs, gr, gls, glr,
):
    t = lax.axis_index("tm")
    b = lax.axis_index("band")
    rows, cols, chans = feats.shape[1:]
    slots = [k for k in range(K) if DISTANCES[k] < nt]
    chained = 2 in slots and 3 in slots
    near, far = 2, 3
    log_chunks = (H * J) // CHUNK

    barrier = pltpu.get_barrier_semaphore()

    def greet_t(i, c):
        pl.semaphore_signal(barrier, inc=1, device_id=(lax.rem(t + i, nt), b), device_id_type=MESH)
        return c

    def greet_b(i, c):
        pl.semaphore_signal(barrier, inc=1, device_id=(t, lax.rem(b + i, nb)), device_id_type=MESH)
        return c

    lax.fori_loop(1, nt, greet_t, 0)
    lax.fori_loop(1, nb, greet_b, 0)

    def rc(src, dst, ss, rs, tt, bb):
        return pltpu.make_async_remote_copy(
            src_ref=src, dst_ref=dst, send_sem=ss, recv_sem=rs, device_id=(tt, bb), device_id_type=MESH
        )

    def loop(body):
        def step(r, c):
            body(r)
            return c

        lax.fori_loop(0, rows, step, 0)

    def make_values(r):
        val[r] = nt_dot(w_value_t[...], feats[0, r]).astype(BF16)

    loop(make_values)
    pl.semaphore_wait(barrier, nt - 1 + nb - 1)

    def hop(k):
        return DISTANCES[near] if chained and k == far else DISTANCES[k]

    def main_of(k):
        return ext.at[k, pl.ds(1, rows)]

    def fwd(k):
        src = main_of(near) if chained and k == far else val
        return rc(src, main_of(k), fs.at[k], fr.at[k], lax.rem(t + hop(k), nt), b)

    def sends_fwd(k):
        if chained and k == far:
            return (t >= DISTANCES[near]) & (t + DISTANCES[near] < nt)
        return t + DISTANCES[k] < nt

    order = [k for k in (2, 1, 0, 4) if k in slots]
    for k in order:
        @pl.when(sends_fwd(k))
        def _(k=k):
            fwd(k).start()

    def make_attn(r):
        dmix[r] = nt_dot(w_out[...], cot[0, r]).astype(BF16)
        logits = nt_dot(wl_t[...], feats[0, r])
        ls = [logits[0:H]]
        oks = [None]
        for k in slots:
            flag = present[0, k] * jnp.where(t >= DISTANCES[k], 1, 0)
            ok = jnp.full((H, cols), flag, jnp.int32) == 1
            oks.append(ok)
            ls.append(jnp.where(ok, logits[H * (k + 1) : H * (k + 2)], F32(-1e30)))
        top = functools.reduce(jnp.maximum, ls)
        es = []
        for ok, l in zip(oks, ls):
            e = jnp.exp(l - top)
            es.append(e if ok is None else jnp.where(ok, e, F32(0.0)))
        total = functools.reduce(jnp.add, es)
        for j in range(len(es)):
            attn[r, j] = es[j] / total

    loop(make_attn)

    def low(r, j):
        return spread_heads(attn[r, j].astype(BF16).astype(F32))

    def rim(k, side):
        other = b - 1 if side == 0 else b + 1
        return rc(rim_out.at[k, side], rim_in.at[k, 1 - side], ms.at[k, side], mr.at[k, 1 - side],
                  t, lax.rem(other + nb, nb))

    def has(side):
        return b > 0 if side == 0 else b < nb - 1

    def contribute(k):
        acc[k] = jnp.zeros_like(acc[k])

        def body(r):
            delta = lax.broadcasted_iota(jnp.int32, (cols, cols), 0) - lax.broadcasted_iota(jnp.int32, (cols, cols), 1)
            up = row_off[0, k, pl.ds(r, 1), :] < 0
            u = delta - col_off[0, k, pl.ds(r, 1), :]
            fa = frac[0, 0, k, pl.ds(r, 1), :].astype(F32)
            fb = frac[0, 1, k, pl.ds(r, 1), :].astype(F32)
            wc = jnp.where(u == 0, 8.0 - fb, jnp.where(u == 1, fb, F32(0.0)))
            first = (8.0 - fa) / 64.0
            second = fa / 64.0
            weights = (jnp.where(up, first, F32(0.0)), jnp.where(up, second, first), jnp.where(up, F32(0.0), second))
            table = jnp.concatenate([(wc * w).astype(BF16) for w in weights], axis=0)
            tables[k, r] = table
            ds = (low(r, k + 1) * dmix[r].astype(F32)).astype(BF16)
            part = nt_dot(ds, table)
            for d in range(3):
                acc[k, r + d] += part[:, d * cols : (d + 1) * cols]

        loop(body)
        for side in (0, 1):
            rim_out[k, side] = acc[k, 0 if side == 0 else rows + 1].astype(BF16)

            @pl.when(has(side))
            def _(side=side):
                rim(k, side).start()

    def bwd(k):
        return rc(cout.at[k], cin.at[k], bs.at[k], br.at[k], lax.rem(t - hop(k) + nt, nt), b)

    def sends_bwd(k):
        return t >= DISTANCES[k]

    def gets_bwd(k):
        if chained and k == far:
            return (t >= DISTANCES[near]) & (t + DISTANCES[near] < nt)
        return t + DISTANCES[k] < nt

    def finish_contribution(k):
        for side in (0, 1):
            @pl.when(has(side))
            def _(side=side):
                rim(k, 1 - side).wait_recv()
                row = 1 if side == 0 else rows
                acc[k, row] += rim_in[k, side].astype(F32)

        if chained and k == near:
            @pl.when(gets_bwd(far))
            def _():
                bwd(far).wait_recv()

                def body(r):
                    acc[k, r + 1] += cin[far, r].astype(F32)

                loop(body)

        def body(r):
            cout[k, r] = acc[k, r + 1].astype(BF16)

        loop(body)

        @pl.when(sends_bwd(k))
        def _():
            bwd(k).start()

    back_order = [k for k in (3, 1, 0, 2, 4) if k in slots]
    late = [near] if chained else []
    previous = None
    for k in back_order:
        contribute(k)
        if previous is not None:
            finish_contribution(previous)
        previous = None if k in late else k
    if previous is not None:
        finish_contribution(previous)

    def halo(k, side):
        src = ext.at[k, 1 if side == 0 else rows]
        dst = ext.at[k, rows + 1 if side == 0 else 0]
        other = b - 1 if side == 0 else b + 1
        return rc(src, dst, hs.at[k, side], hr.at[k, 1 - side], t, lax.rem(other + nb, nb))

    def take(k):
        @pl.when(t >= DISTANCES[k])
        def _():
            fwd(k).wait_recv()
            for side in (0, 1):
                @pl.when(has(side))
                def _(side=side):
                    halo(k, side).start()

                @pl.when(jnp.logical_not(has(side)))
                def _(side=side):
                    ext[k, 0 if side == 0 else rows + 1] = jnp.zeros((chans, cols), BF16)

        @pl.when(t < DISTANCES[k])
        def _():
            ext[k] = jnp.zeros_like(ext[k])

    def clear_mix(r):
        s = val[r].astype(F32)
        mix[r] = low(r, 0) * s
        dattn[r, 0] = head_sums(dmix[r].astype(F32) * s)

    def sample(k):
        for side in (0, 1):
            @pl.when((t >= DISTANCES[k]) & has(side))
            def _(side=side):
                halo(k, 1 - side).wait_recv()

        def body(r):
            v = jnp.concatenate([ext[k, r], ext[k, r + 1], ext[k, r + 2]], axis=1)
            s = dot(v, tables[k, r]).astype(BF16).astype(F32)
            mix[r] += low(r, k + 1) * s
            dattn[r, k + 1] = head_sums(dmix[r].astype(F32) * s)

        loop(body)

    if chained:
        take(near)

        @pl.when(sends_fwd(far))
        def _():
            fwd(far).start()

    loop(clear_mix)
    for k in order:
        if not (chained and k == near):
            take(k)
    for k in late:
        finish_contribution(k)
    for k in order:
        sample(k)
    if far in slots:
        take(far)
        sample(far)

    g_out[...] = jnp.zeros_like(g_out)
    g_val[...] = jnp.zeros_like(g_val)
    g_log[...] = jnp.zeros_like(g_log)
    used = len(slots) + 1

    def finish_attn(r):
        ats = [attn[r, j] for j in range(used)]
        das = [dattn[r, j] for j in range(used)]
        inner = functools.reduce(jnp.add, [a * d for a, d in zip(ats, das)])
        dls = [a * (d - inner) for a, d in zip(ats, das)]
        dls += [jnp.zeros((H, cols), F32)] * (J - used)
        dl = jnp.concatenate(dls, axis=0).astype(BF16)
        dlog[r] = dl
        g_log[...] += dot(dl, feats[0, r])
        g_out[...] += dot(mix[r].astype(BF16), cot[0, r])

    loop(finish_attn)

    def peers(body):
        def step(i, c):
            body(lax.rem(t + i, nt))
            return c

        lax.fori_loop(1, nt, step, 0)

    def part(o):
        return pl.ds(pl.multiple_of(o * CHUNK, CHUNK), CHUNK)

    def scatter(src, dst, ss, rs, to, sender):
        return rc(src.at[part(to)], dst.at[sender], ss.at[to], rs.at[sender], to, b)

    s_out[...] = g_out[...].astype(BF16)
    s_log[...] = g_log[...].astype(BF16)

    def send_first(o):
        @pl.when(o < owners)
        def _():
            scatter(s_out, r_out, ros, ror, o, t).start()

        @pl.when(o < log_chunks)
        def _():
            scatter(s_log, r_log, rls, rlr, o, t).start()

    peers(send_first)

    for k in slots:
        if not (chained and k == far):
            @pl.when(gets_bwd(k))
            def _(k=k):
                bwd(k).wait_recv()

            @pl.when(jnp.logical_not(gets_bwd(k)))
            def _(k=k):
                cin[k] = jnp.zeros_like(cin[k])

    def finish_values(r):
        total = (low(r, 0) * dmix[r].astype(F32)).astype(BF16).astype(F32)
        for k in slots:
            if not (chained and k == far):
                total = total + cin[k, r].astype(F32)
        dv = total.astype(BF16)
        val[r] = dv
        g_val[...] += dot(dv, feats[0, r])

    for k in order:
        @pl.when(sends_fwd(k))
        def _(k=k):
            fwd(k).wait_send()

    loop(finish_values)
    s_val[...] = g_val[...].astype(BF16)

    def send_second(o):
        @pl.when(o < owners)
        def _():
            scatter(s_val, r_val, rvs, rvr, o, t).start()

    peers(send_second)

    def finish_feats(r):
        g = dot(w_value[...], val[r]) + dot(wl[...], dlog[r])
        out_feats[0, r] = (cot[0, r].astype(F32) + g.T).astype(BF16)

    loop(finish_feats)

    @pl.when(t < owners)
    def _():
        def reduce_one(src, got, rs, at):
            def body(i, total):
                p = lax.rem(t + i, nt)
                rc(got.at[p], got.at[p], rs.at[p], rs.at[p], p, b).wait_recv()
                return total + got[p].astype(F32)

            total = lax.fori_loop(1, nt, body, src[part(t), :])
            band_part[b, at] = total.astype(BF16)

        reduce_one(g_out, r_out, ror, 0)
        reduce_one(g_val, r_val, rvr, 1)

        @pl.when(t < log_chunks)
        def _():
            reduce_one(g_log, r_log, rlr, 2)

        @pl.when(t >= log_chunks)
        def _():
            band_part[b, 2] = jnp.zeros((CHUNK, chans), BF16)

        def swap(i):
            to = lax.rem(b + i, nb)
            return rc(band_part.at[b], band_part.at[b], xs.at[to], xr.at[b], t, to)

        def got(i):
            frm = lax.rem(b + i, nb)
            return rc(band_part.at[frm], band_part.at[frm], xs.at[frm], xr.at[frm], t, frm)

        def start(i, c):
            swap(i).start()
            return c

        def finish(i, c):
            got(i).wait_recv()
            return c

        lax.fori_loop(1, nb, start, 0)
        lax.fori_loop(1, nb, finish, 0)
        total = band_part[0].astype(F32)
        for i in range(1, nb):
            total = total + band_part[i].astype(F32)
        whole[...] = total.astype(BF16)
        gathered[t] = whole[...]

        def spread(p):
            rc(whole.at[pl.ds(0, 2)], gathered.at[t, pl.ds(0, 2)], gs.at[p], gr.at[t], p, b).start()

            @pl.when(t < log_chunks)
            def _():
                rc(whole.at[2], gathered.at[t, 2], gls.at[p], glr.at[t], p, b).start()

        peers(spread)

        def swapped(i, c):
            swap(i).wait_send()
            return c

        lax.fori_loop(1, nb, swapped, 0)

    def collect(p):
        @pl.when(p < owners)
        def _():
            rc(whole.at[pl.ds(0, 2)], gathered.at[p, pl.ds(0, 2)], gs.at[p], gr.at[p], p, b).wait_recv()

        @pl.when(p < log_chunks)
        def _():
            rc(whole.at[2], gathered.at[p, 2], gls.at[p], glr.at[p], p, b).wait_recv()

    peers(collect)

    for o in range(owners):
        out_wout[o * CHUNK : (o + 1) * CHUNK, :] = gathered[o, 0].astype(F32)
        g_val[o * CHUNK : (o + 1) * CHUNK, :] = gathered[o, 1].astype(F32)
    for o in range(log_chunks):
        out_logit[o * CHUNK : (o + 1) * CHUNK, :] = gathered[o, 2].astype(F32)
    out_value[...] = g_val[...].T

    def drain(p):
        @pl.when(p < owners)
        def _():
            scatter(s_out, r_out, ros, ror, p, t).wait_send()
            scatter(s_val, r_val, rvs, rvr, p, t).wait_send()

        @pl.when(p < log_chunks)
        def _():
            scatter(s_log, r_log, rls, rlr, p, t).wait_send()

        @pl.when(t < owners)
        def _():
            rc(whole.at[pl.ds(0, 2)], gathered.at[t, pl.ds(0, 2)], gs.at[p], gr.at[t], p, b).wait_send()

        @pl.when(t < log_chunks)
        def _():
            rc(whole.at[2], gathered.at[t, 2], gls.at[p], glr.at[t], p, b).wait_send()

    peers(drain)
    for k in slots:
        if chained and k == far:
            @pl.when(sends_fwd(k))
            def _(k=k):
                fwd(k).wait_send()

        @pl.when(sends_bwd(k))
        def _(k=k):
            bwd(k).wait_send()

        for side in (0, 1):
            @pl.when(has(side))
            def _(k=k, side=side):
                rim(k, side).wait_send()

            @pl.when((t >= DISTANCES[k]) & has(side))
            def _(k=k, side=side):
                halo(k, side).wait_send()


def shards(nt, nb, feats, cotangent, w_value, w_logit, w_out, row_offsets, col_offsets, fractions, present):
    rows, cols, chans = feats.shape[1:]
    owners = chans // CHUNK
    wl = w_logit.reshape(chans, H, J).transpose(0, 2, 1).reshape(chans, H * J)
    vmem = pl.BlockSpec(memory_space=pltpu.VMEM)
    slots = sum(1 for d in DISTANCES if d < nt)
    grid = (rows, chans, cols)
    dma = pltpu.SemaphoreType.DMA
    v = pltpu.VMEM
    square = (chans, chans)
    logs = (H * J, chans)
    landing = (nt, CHUNK, chans)
    scratch = [
        v(grid, BF16),
        v((slots, rows + 2, chans, cols), BF16),
        v((slots, rows, 3 * cols, cols), BF16),
        v((rows, slots + 1, H, cols), F32),
        v(grid, BF16),
        v((rows, slots + 1, H, cols), F32),
        v(grid, F32),
        v((rows, H * J, cols), BF16),
        v((slots, rows + 2, chans, cols), F32),
        v((slots,) + grid, BF16),
        v((slots,) + grid, BF16),
        v((slots, 2, chans, cols), BF16),
        v((slots, 2, chans, cols), BF16),
        v(square, F32), v(square, F32), v(logs, F32),
        v(square, BF16), v(square, BF16), v(logs, BF16),
        v(landing, BF16), v(landing, BF16), v(landing, BF16),
        v((nb, 3, CHUNK, chans), BF16),
        v((3, CHUNK, chans), BF16),
        v((nt, 3, CHUNK, chans), BF16),
        dma((slots,)), dma((slots,)),
        dma((slots, 2)), dma((slots, 2)),
        dma((slots,)), dma((slots,)),
        dma((slots, 2)), dma((slots, 2)),
        dma((nt,)), dma((nt,)), dma((nt,)), dma((nt,)), dma((nt,)), dma((nt,)),
        dma((nb,)), dma((nb,)),
        dma((nt,)), dma((nt,)), dma((nt,)), dma((nt,)),
    ]
    grad_feats, g_value, g_logit, g_out = pl.pallas_call(
        functools.partial(kernel, nt, nb, owners),
        out_shape=(
            jax.ShapeDtypeStruct(feats.shape, BF16),
            jax.ShapeDtypeStruct(square, F32),
            jax.ShapeDtypeStruct(logs, F32),
            jax.ShapeDtypeStruct(square, F32),
        ),
        in_specs=[vmem] * 10 + [pl.BlockSpec(memory_space=pltpu.SMEM)],
        out_specs=(vmem,) * 4,
        scratch_shapes=scratch,
        compiler_params=pltpu.CompilerParams(
            collective_id=0, has_side_effects=True, vmem_limit_bytes=56 * 1024 * 1024
        ),
    )(feats, cotangent, w_value, w_value.T, w_out, wl.T, wl, row_offsets, col_offsets, fractions, present)
    g_logit = g_logit.reshape(J, H, chans).transpose(2, 1, 0).reshape(chans, H * J)
    return grad_feats, g_value, g_logit, g_out


def solution(mesh):
    placed = (
        P("tm", "band", None, None),
        P("tm", "band", None, None),
        P(),
        P(),
        P(),
        P("tm", None, "band", None),
        P("tm", None, "band", None),
        P("tm", None, None, "band", None),
        P("tm", None),
    )
    return jax.shard_map(
        functools.partial(shards, mesh.shape["tm"], mesh.shape["band"]),
        mesh=mesh,
        in_specs=placed,
        out_specs=(P("tm", "band", None, None), P(), P(), P()),
        check_vma=False,
    )
```

time: 382 us -> 85 us (0.22)
  waiting for transfers between devices: 183 us -> 0 us
  Pallas kernels: 0 us -> 76.7 us
  blocking collectives: 56.9 us -> 0 us
  matrix products: 46.7 us -> 0 us
  starting transfers between devices: 43.5 us -> 0 us
  between operations: 19 us -> 0.67 us
  local copies, waits for them, and re-layouts: 24.5 us -> 7.41 us
  other arithmetic: 7.31 us -> 0 us
    psum x1 -> x0, waiting for transfers between devices: 153 us -> none  [shards(): summed = lax.psum((local_value, local_logit, local_out), ('tm', 'band'))]
    pallas_call x0 -> x1, Pallas kernels: none -> 76.7 us  [shards(): pl.pallas_call(functools.partial(kernel, nt, nb, owners), out_shape=(jax....]
    psum x1 -> x0, blocking collectives: 56.9 us -> none  [shards(): summed = lax.psum((local_value, local_logit, local_out), ('tm', 'band'))]
    dot_general x18 -> x0, matrix products: 46.7 us -> none  [the longest x8 23.5 us: transposed_product(): lax.dot_general(table, operand, (((0,), (0,)), ((), ())), preferred_eleme...]
    ppermute x19 -> x0, starting transfers between devices: 43.5 us -> none  [the longest x17 37.4 us: shifted(): lax.ppermute(value, axis, [(source, source + steps) for source in range(i...]
    ppermute x19 -> x0, waiting for transfers between devices: 29.5 us -> none  [the longest x17 24.7 us: shifted(): lax.ppermute(value, axis, [(source, source + steps) for source in range(i...]
    ppermute x5 -> x0, local copies, waits for them, and re-layouts: 6.78 us -> none  [shifted(): lax.ppermute(value, axis, [(source, source + steps) for source in range(i...]
    dot_general x2 -> x0, other arithmetic: 6.27 us -> none  [the longest x1 3.57 us: shards(): jnp.einsum('qhe,jqhe->qhj', d_heads, stacked, preferred_element_type=jnp....]
  transfers between devices with their start and end apart: 20 -> 0, of which waited for: 8 -> 0; matrix products, arithmetic and copies ran while one was open for 15% -> 0% of each run, Pallas kernels for 0% -> 0%
where the time goes in v1:
time: 85 us; the launch traced here: 84.7 us
  Pallas kernels  76.7 us (90%)
  local copies, waits for them, and re-layouts  7.41 us (9%)
    pallas_call x1, Pallas kernels, shards(): pl.pallas_call(functools.partial(kernel, nt, nb, owners), out_shape=(jax....  76.7 us
    unnamed x12, local copies, waits for them, and re-layouts  4.43 us

profile of v1, /device:TPU:0, one launch (start us, length us, event | category | flops | bytes accessed | tf_op | source)
XLA Modules:
  0.0 84.7 jit_solution(5564350121858600120)
XLA Ops:
  0.6 0.0 copy-start
  0.6 0.8 reshape.20
  1.4 0.0 copy-start.3
  1.5 0.7 copy.19.wl
  2.2 0.0 copy-done.3
  2.2 0.0 copy-done
  2.2 0.8 copy.17
  3.0 76.7 %shard_map.120 = (bf16[1,8,128,256]{3,2,1,0:T(8,128)(2,1)}, f32[256,256]{1,0:T(8,128)}, f32[48,256]{1,0:T(8,128)}, f32[256,256]{1,0:T(8,128)}) custom-call(bf16[1,8,128,256]{3,2,1,0:T(8,128)(2,1)} %feats.1, bf16[1,8,128,256]{3,2,1,0:T(8,128)(2,1)} %cot.1, bf16[256,256]{1,0:T(8,128)(2,1)} %w_value.1, bf16[256,256]{1,0:T(8,128)(2,1)} %bitcast.16, ...), custom_call_target="tpu_custom_call" | custom-call | tf_op jit(solution)/shard_map/pallas_call | solution.py:519
  79.6 0.8 copy.24
  80.4 0.6 reshape.23
  81.1 0.0 copy-start.2
  81.1 1.9 %copy.29 = bf16[1,8,128,256]{3,2,1,0:T(8,128)(2,1)} copy(bf16[1,8,128,256]{3,2,1,0:T(8,128)(2,1)} %get-tuple-element.18) | data formatting | bytes 1048576
  83.0 0.0 copy-done.2
  83.0 0.0 copy-start.1
  83.0 0.7 copy.30
  83.7 0.3 copy-done.1
  84.0 0.7 copy.31
  (1 shorter events, 0.0 us)
Async XLA Ops:
  0.6 1.6 %copy-start = (bf16[256,256]{1,0:T(8,128)(2,1)S(1)}, bf16[256,256]{1,0:T(8,128)(2,1)}, u32[]{:S(2)}) copy-start(bf16[256,256]{1,0:T(8,128)(2,1)} %w_value.1) | copy-start | bytes 393220
  1.4 0.7 copy-start.3
  81.1 1.9 %copy-start.2 = (f32[256,256]{1,0:T(8,128)S(1)}, f32[256,256]{1,0:T(8,128)}, u32[]{:S(2)}) copy-start(f32[256,256]{1,0:T(8,128)} %get-tuple-element.19) | copy-start | bytes 786436
  83.0 1.0 %copy-start.1 = (f32[256,256]{1,0:T(8,128)S(1)}, f32[256,256]{1,0:T(8,128)}, u32[]{:S(2)}) copy-start(f32[256,256]{1,0:T(8,128)} %get-tuple-element.21) | copy-start | bytes 786436

commit v2 on v1

--- a/solution.py
+++ b/solution.py
@@ -26,6 +26,12 @@
     return jnp.dot(a, b, preferred_element_type=F32)
 
 
+def entry_order(axis):
+    mine = lax.broadcasted_iota(jnp.int32, (H * J, H * J), axis)
+    theirs = lax.broadcasted_iota(jnp.int32, (H * J, H * J), 1 - axis)
+    return jnp.where(theirs == (mine & (H - 1)) * J + (mine >> 3), F32(1.0), F32(0.0)).astype(BF16)
+
+
 def spread_heads(a):
     return jnp.concatenate([jnp.broadcast_to(a[h : h + 1], (E, a.shape[1])) for h in range(H)], axis=0)
 
@@ -36,9 +42,9 @@
 
 def kernel(
     nt, nb, owners,
-    feats, cot, w_value, w_value_t, w_out, wl_t, wl, row_off, col_off, frac, present,
-    out_feats, out_value, out_logit, out_wout,
-    val, ext, tables, attn, dmix, dattn, mix, dlog, acc, cout, cin, rim_out, rim_in,
+    feats, cot, w_value, w_logit, w_out, row_off, col_off, frac, present,
+    out_feats, out_sums, out_logs,
+    w_value_t, wl_t, wl, val, ext, tables, attn, dmix, dattn, mix, dlog, dval, acc, cout, cin, rim_out, rim_in,
     g_out, g_val, g_log, s_out, s_val, s_log, r_out, r_val, r_log,
     band_part, whole, gathered,
     fs, fr, hs, hr, bs, br, ms, mr, ros, ror, rvs, rvr, rls, rlr, xs, xr, gs, gr, gls, glr,
@@ -70,16 +76,27 @@
         )
 
     def loop(body):
-        def step(r, c):
+        for r in range(rows):
             body(r)
-            return c
-
-        lax.fori_loop(0, rows, step, 0)
-
-    def make_values(r):
-        val[r] = nt_dot(w_value_t[...], feats[0, r]).astype(BF16)
-
-    loop(make_values)
+
+    def pairs(body):
+        for p in range(rows // 2):
+            body(p, slice(2 * p * cols, (2 * p + 2) * cols))
+
+    def cells(ref, p):
+        return ref[0, 2 * p : 2 * p + 2].reshape(2 * cols, chans)
+
+    w_value_t[...] = w_value[...].astype(F32).T.astype(BF16)
+    order_in = entry_order(0)
+    wl_t[...] = nt_dot(order_in, w_logit[...]).astype(BF16)
+    wl[...] = nt_dot(w_logit[...], order_in).astype(BF16)
+
+    def make_values(p, at):
+        v = nt_dot(w_value_t[...], cells(feats, p)).astype(BF16)
+        val[2 * p] = v[:, :cols]
+        val[2 * p + 1] = v[:, cols:]
+
+    pairs(make_values)
     pl.semaphore_wait(barrier, nt - 1 + nb - 1)
 
     def hop(k):
@@ -103,14 +120,14 @@
         def _(k=k):
             fwd(k).start()
 
-    def make_attn(r):
-        dmix[r] = nt_dot(w_out[...], cot[0, r]).astype(BF16)
-        logits = nt_dot(wl_t[...], feats[0, r])
+    def make_attn(p, at):
+        dmix[:, at] = nt_dot(w_out[...], cells(cot, p)).astype(BF16)
+        logits = nt_dot(wl_t[...], cells(feats, p))
         ls = [logits[0:H]]
         oks = [None]
         for k in slots:
             flag = present[0, k] * jnp.where(t >= DISTANCES[k], 1, 0)
-            ok = jnp.full((H, cols), flag, jnp.int32) == 1
+            ok = jnp.full((H, 2 * cols), flag, jnp.int32) == 1
             oks.append(ok)
             ls.append(jnp.where(ok, logits[H * (k + 1) : H * (k + 2)], F32(-1e30)))
         top = functools.reduce(jnp.maximum, ls)
@@ -120,12 +137,12 @@
             es.append(e if ok is None else jnp.where(ok, e, F32(0.0)))
         total = functools.reduce(jnp.add, es)
         for j in range(len(es)):
-            attn[r, j] = es[j] / total
-
-    loop(make_attn)
-
-    def low(r, j):
-        return spread_heads(attn[r, j].astype(BF16).astype(F32))
+            attn[j, :, at] = es[j] / total
+
+    pairs(make_attn)
+
+    def low(j, at):
+        return spread_heads(attn[j, :, at].astype(BF16).astype(F32))
 
     def rim(k, side):
         other = b - 1 if side == 0 else b + 1
@@ -136,26 +153,36 @@
         return b > 0 if side == 0 else b < nb - 1
 
     def contribute(k):
-        acc[k] = jnp.zeros_like(acc[k])
-
-        def body(r):
-            delta = lax.broadcasted_iota(jnp.int32, (cols, cols), 0) - lax.broadcasted_iota(jnp.int32, (cols, cols), 1)
-            up = row_off[0, k, pl.ds(r, 1), :] < 0
-            u = delta - col_off[0, k, pl.ds(r, 1), :]
-            fa = frac[0, 0, k, pl.ds(r, 1), :].astype(F32)
-            fb = frac[0, 1, k, pl.ds(r, 1), :].astype(F32)
+        delta = lax.broadcasted_iota(jnp.int32, (cols, cols), 0) - lax.broadcasted_iota(jnp.int32, (cols, cols), 1)
+
+        def one_row(r):
+            up = row_off[0, k, r : r + 1, :] < 0
+            u = delta - col_off[0, k, r : r + 1, :]
+            fa = frac[0, 0, k, r : r + 1, :].astype(F32)
+            fb = frac[0, 1, k, r : r + 1, :].astype(F32)
             wc = jnp.where(u == 0, 8.0 - fb, jnp.where(u == 1, fb, F32(0.0)))
             first = (8.0 - fa) / 64.0
             second = fa / 64.0
             weights = (jnp.where(up, first, F32(0.0)), jnp.where(up, second, first), jnp.where(up, F32(0.0), second))
-            table = jnp.concatenate([(wc * w).astype(BF16) for w in weights], axis=0)
-            tables[k, r] = table
-            ds = (low(r, k + 1) * dmix[r].astype(F32)).astype(BF16)
+            return [(wc * w).astype(BF16) for w in weights]
+
+        empty = jnp.zeros((cols, cols), BF16)
+
+        def body(p, at):
+            left = jnp.concatenate(one_row(2 * p) + [empty], axis=0)
+            right = jnp.concatenate([empty] + one_row(2 * p + 1), axis=0)
+            table = jnp.concatenate([left, right], axis=1)
+            tables[k, p] = table
+            ds = (low(k + 1, at) * dmix[:, at].astype(F32)).astype(BF16)
             part = nt_dot(ds, table)
-            for d in range(3):
-                acc[k, r + d] += part[:, d * cols : (d + 1) * cols]
-
-        loop(body)
+            for d in range(4):
+                piece = part[:, d * cols : (d + 1) * cols]
+                if d < 2 and p > 0:
+                    acc[k, 2 * p + d] += piece
+                else:
+                    acc[k, 2 * p + d] = piece
+
+        pairs(body)
         for side in (0, 1):
             rim_out[k, side] = acc[k, 0 if side == 0 else rows + 1].astype(BF16)
 
@@ -235,10 +262,10 @@
         def _():
             ext[k] = jnp.zeros_like(ext[k])
 
-    def clear_mix(r):
-        s = val[r].astype(F32)
-        mix[r] = low(r, 0) * s
-        dattn[r, 0] = head_sums(dmix[r].astype(F32) * s)
+    def own_sample(p, at):
+        s = jnp.concatenate([val[2 * p], val[2 * p + 1]], axis=1).astype(F32)
+        mix[:, at] = low(0, at) * s
+        dattn[0, :, at] = head_sums(dmix[:, at].astype(F32) * s)
 
     def sample(k):
         for side in (0, 1):
@@ -246,13 +273,13 @@
             def _(side=side):
                 halo(k, 1 - side).wait_recv()
 
-        def body(r):
-            v = jnp.concatenate([ext[k, r], ext[k, r + 1], ext[k, r + 2]], axis=1)
-            s = dot(v, tables[k, r]).astype(BF16).astype(F32)
-            mix[r] += low(r, k + 1) * s
-            dattn[r, k + 1] = head_sums(dmix[r].astype(F32) * s)
-
-        loop(body)
+        def body(p, at):
+            v = jnp.concatenate([ext[k, 2 * p + d] for d in range(4)], axis=1)
+            s = dot(v, tables[k, p]).astype(BF16).astype(F32)
+            mix[:, at] += low(k + 1, at) * s
+            dattn[k + 1, :, at] = head_sums(dmix[:, at].astype(F32) * s)
+
+        pairs(body)
 
     if chained:
         take(near)
@@ -261,7 +288,7 @@
         def _():
             fwd(far).start()
 
-    loop(clear_mix)
+    pairs(own_sample)
     for k in order:
         if not (chained and k == near):
             take(k)
@@ -273,23 +300,23 @@
         take(far)
         sample(far)
 
-    g_out[...] = jnp.zeros_like(g_out)
-    g_val[...] = jnp.zeros_like(g_val)
-    g_log[...] = jnp.zeros_like(g_log)
     used = len(slots) + 1
 
-    def finish_attn(r):
-        ats = [attn[r, j] for j in range(used)]
-        das = [dattn[r, j] for j in range(used)]
+    def finish_attn(p, at):
+        ats = [attn[j, :, at] for j in range(used)]
+        das = [dattn[j, :, at] for j in range(used)]
         inner = functools.reduce(jnp.add, [a * d for a, d in zip(ats, das)])
         dls = [a * (d - inner) for a, d in zip(ats, das)]
-        dls += [jnp.zeros((H, cols), F32)] * (J - used)
-        dl = jnp.concatenate(dls, axis=0).astype(BF16)
-        dlog[r] = dl
-        g_log[...] += dot(dl, feats[0, r])
-        g_out[...] += dot(mix[r].astype(BF16), cot[0, r])
-
-    loop(finish_attn)
+        dls += [jnp.zeros((H, 2 * cols), F32)] * (J - used)
+        dlog[:, at] = jnp.concatenate(dls, axis=0).astype(BF16)
+
+    pairs(finish_attn)
+
+    def all_cells(ref):
+        return ref[0].reshape(rows * cols, chans)
+
+    g_log[...] = dot(dlog[...], all_cells(feats))
+    g_out[...] = dot(mix[...].astype(BF16), all_cells(cot))
 
     def peers(body):
         def step(i, c):
@@ -328,21 +355,20 @@
             def _(k=k):
                 cin[k] = jnp.zeros_like(cin[k])
 
-    def finish_values(r):
-        total = (low(r, 0) * dmix[r].astype(F32)).astype(BF16).astype(F32)
+    def finish_values(p, at):
+        total = (low(0, at) * dmix[:, at].astype(F32)).astype(BF16).astype(F32)
         for k in slots:
             if not (chained and k == far):
-                total = total + cin[k, r].astype(F32)
-        dv = total.astype(BF16)
-        val[r] = dv
-        g_val[...] += dot(dv, feats[0, r])
+                total = total + jnp.concatenate([cin[k, 2 * p], cin[k, 2 * p + 1]], axis=1).astype(F32)
+        dval[:, at] = total.astype(BF16)
 
     for k in order:
         @pl.when(sends_fwd(k))
         def _(k=k):
             fwd(k).wait_send()
 
-    loop(finish_values)
+    pairs(finish_values)
+    g_val[...] = dot(dval[...], all_cells(feats))
     s_val[...] = g_val[...].astype(BF16)
 
     def send_second(o):
@@ -352,11 +378,12 @@
 
     peers(send_second)
 
-    def finish_feats(r):
-        g = dot(w_value[...], val[r]) + dot(wl[...], dlog[r])
-        out_feats[0, r] = (cot[0, r].astype(F32) + g.T).astype(BF16)
-
-    loop(finish_feats)
+    def finish_feats(p, at):
+        g = dot(w_value[...], dval[:, at]) + dot(wl[...], dlog[:, at])
+        done = (cells(cot, p).astype(F32) + g.T).astype(BF16)
+        out_feats[0, 2 * p : 2 * p + 2] = done.reshape(2, cols, chans)
+
+    pairs(finish_feats)
 
     @pl.when(t < owners)
     def _():
@@ -430,12 +457,9 @@
 
     peers(collect)
 
-    for o in range(owners):
-        out_wout[o * CHUNK : (o + 1) * CHUNK, :] = gathered[o, 0].astype(F32)
-        g_val[o * CHUNK : (o + 1) * CHUNK, :] = gathered[o, 1].astype(F32)
-    for o in range(log_chunks):
-        out_logit[o * CHUNK : (o + 1) * CHUNK, :] = gathered[o, 2].astype(F32)
-    out_value[...] = g_val[...].T
+    for i in (0, 1):
+        out_sums[i] = gathered[:owners, i].reshape(chans, chans)
+    out_logs[...] = gathered[:log_chunks, 2].reshape(H * J, chans)
 
     def drain(p):
         @pl.when(p < owners)
@@ -476,10 +500,16 @@
                 halo(k, side).wait_send()
 
 
+def unpack(feats, sums, logs, out_feats, out_value, out_logit, out_wout):
+    out_feats[...] = feats[...]
+    out_wout[...] = sums[0].astype(F32)
+    out_value[...] = sums[1].astype(F32).T
+    out_logit[...] = dot(entry_order(1), logs[...]).T
+
+
 def shards(nt, nb, feats, cotangent, w_value, w_logit, w_out, row_offsets, col_offsets, fractions, present):
     rows, cols, chans = feats.shape[1:]
     owners = chans // CHUNK
-    wl = w_logit.reshape(chans, H, J).transpose(0, 2, 1).reshape(chans, H * J)
     vmem = pl.BlockSpec(memory_space=pltpu.VMEM)
     slots = sum(1 for d in DISTANCES if d < nt)
     grid = (rows, chans, cols)
@@ -488,15 +518,18 @@
     square = (chans, chans)
     logs = (H * J, chans)
     landing = (nt, CHUNK, chans)
+    flat = (chans, rows * cols)
     scratch = [
+        v(square, BF16), v(logs, BF16), v(logs[::-1], BF16),
         v(grid, BF16),
         v((slots, rows + 2, chans, cols), BF16),
-        v((slots, rows, 3 * cols, cols), BF16),
-        v((rows, slots + 1, H, cols), F32),
-        v(grid, BF16),
-        v((rows, slots + 1, H, cols), F32),
-        v(grid, F32),
-        v((rows, H * J, cols), BF16),
+        v((slots, rows // 2, 4 * cols, 2 * cols), BF16),
+        v((slots + 1, H, rows * cols), F32),
+        v(flat, BF16),
+        v((slots + 1, H, rows * cols), F32),
+        v(flat, F32),
+        v((H * J, rows * cols), BF16),
+        v(flat, BF16),
         v((slots, rows + 2, chans, cols), F32),
         v((slots,) + grid, BF16),
         v((slots,) + grid, BF16),
@@ -516,23 +549,27 @@
         dma((nb,)), dma((nb,)),
         dma((nt,)), dma((nt,)), dma((nt,)), dma((nt,)),
     ]
-    grad_feats, g_value, g_logit, g_out = pl.pallas_call(
+    grad_feats, sums, log_sums = pl.pallas_call(
         functools.partial(kernel, nt, nb, owners),
-        out_shape=(
-            jax.ShapeDtypeStruct(feats.shape, BF16),
-            jax.ShapeDtypeStruct(square, F32),
-            jax.ShapeDtypeStruct(logs, F32),
-            jax.ShapeDtypeStruct(square, F32),
-        ),
-        in_specs=[vmem] * 10 + [pl.BlockSpec(memory_space=pltpu.SMEM)],
-        out_specs=(vmem,) * 4,
+        out_shape=tuple(jax.ShapeDtypeStruct(shape, BF16) for shape in (feats.shape, (2,) + square, logs)),
+        in_specs=[vmem] * 8 + [pl.BlockSpec(memory_space=pltpu.SMEM)],
+        out_specs=(vmem,) * 3,
         scratch_shapes=scratch,
         compiler_params=pltpu.CompilerParams(
             collective_id=0, has_side_effects=True, vmem_limit_bytes=56 * 1024 * 1024
         ),
-    )(feats, cotangent, w_value, w_value.T, w_out, wl.T, wl, row_offsets, col_offsets, fractions, present)
-    g_logit = g_logit.reshape(J, H, chans).transpose(2, 1, 0).reshape(chans, H * J)
-    return grad_feats, g_value, g_logit, g_out
+    )(feats, cotangent, w_value, w_logit, w_out, row_offsets, col_offsets, fractions, present)
+    return pl.pallas_call(
+        unpack,
+        out_shape=(
+            jax.ShapeDtypeStruct(feats.shape, BF16),
+            jax.ShapeDtypeStruct(square, F32),
+            jax.ShapeDtypeStruct(w_logit.shape, F32),
+            jax.ShapeDtypeStruct(square, F32),
+        ),
+        in_specs=[vmem] * 3,
+        out_specs=(vmem,) * 4,
+    )(grad_feats, sums, log_sums)
 
 
 def solution(mesh):

time: 85 us -> 78 us (0.918)
  local copies, waits for them, and re-layouts: 7.41 us -> 3.07 us
  Pallas kernels: 76.7 us -> 74 us
    reshape x4 -> x0, local copies, waits for them, and re-layouts: 2.97 us -> none  [the longest x2 1.52 us: shards(): wl = w_logit.reshape(chans, H, J).transpose(0, 2, 1).reshape(chans, H * J)]
    unnamed x12 -> x1, local copies, waits for them, and re-layouts: 4.43 us -> 1.47 us
    pallas_call x1 -> x2, Pallas kernels: 76.7 us -> 74 us  [the longest x1 71.8 us: shards(): pl.pallas_call(functools.partial(kernel, nt, nb, owners), out_shape=tuple...]
    pallas_call x0 -> x1, local copies, waits for them, and re-layouts: none -> 1.6 us  [shards(): pl.pallas_call(unpack, out_shape=(jax.ShapeDtypeStruct(feats.shape, BF16)...]
where the time goes in v2:
time: 78 us; the launch traced here: 77.8 us
  Pallas kernels  74 us (95%)
  local copies, waits for them, and re-layouts  3.07 us (4%)
    pallas_call x1, Pallas kernels, shards(): pl.pallas_call(functools.partial(kernel, nt, nb, owners), out_shape=tuple...  71.8 us
    pallas_call x1, Pallas kernels, shards(): pl.pallas_call(unpack, out_shape=(jax.ShapeDtypeStruct(feats.shape, BF16)...  2.23 us
    pallas_call x1, local copies, waits for them, and re-layouts, shards(): pl.pallas_call(unpack, out_shape=(jax.ShapeDtypeStruct(feats.shape, BF16)...  1.6 us

profile of v2, /device:TPU:0, one launch (start us, length us, event | category | flops | bytes accessed | tf_op | source)
XLA Modules:
  0.0 77.8 jit_solution(9936982882317056164)
XLA Ops:
  0.6 1.5 %copy.13.w_logit = bf16[256,48]{1,0:T(8,128)(2,1)} copy(bf16[256,48]{0,1:T(8,128)(2,1)} %param.12) | data formatting | bytes 49152 | tf_op args[3]
  2.1 71.8 %shard_map.120 = (bf16[1,8,128,256]{3,2,1,0:T(8,128)(2,1)}, bf16[2,256,256]{2,1,0:T(8,128)(2,1)}, bf16[48,256]{1,0:T(8,128)(2,1)}) custom-call(bf16[1,8,128,256]{3,2,1,0:T(8,128)(2,1)} %feats.1, bf16[1,8,128,256]{3,2,1,0:T(8,128)(2,1)} %cot.1, bf16[256,256]{1,0:T(8,128)(2,1)} %w_value.1, bf16[256,48]{1,0:T(8,128)(2,1)} %copy.13.w_logit, ...), custom_call_target="tpu_custom_call" | custom-call | tf_op jit(solution)/shard_map/pallas_call | solution.py:552
  73.9 2.2 %shard_map.121 = (bf16[1,8,128,256]{3,2,1,0:T(8,128)(2,1)}, f32[256,256]{1,0:T(8,128)}, f32[256,48]{1,0:T(8,128)}, f32[256,256]{1,0:T(8,128)}) custom-call(bf16[1,8,128,256]{3,2,1,0:T(8,128)(2,1)} %get-tuple-element.7.feats, bf16[2,256,256]{2,1,0:T(8,128)(2,1)} %get-tuple-element.8.sums, bf16[48,256]{1,0:T(8,128)(2,1)} %get-tuple-element.9.logs), custom_call_target="tpu_custom_call" | custom-call | tf_op jit(solution)/shard_map/pallas_call | solution.py:562
  76.2 1.6 %copy.14 = f32[256,48]{0,1:T(8,128)} copy(f32[256,48]{1,0:T(8,128)} %get-tuple-element.12) | data formatting | bytes 98304 | tf_op jit(solution)/shard_map/pallas_call | solution.py:562

commit v3 on v2

--- a/solution.py
+++ b/solution.py
@@ -48,6 +48,7 @@
     g_out, g_val, g_log, s_out, s_val, s_log, r_out, r_val, r_log,
     band_part, whole, gathered,
     fs, fr, hs, hr, bs, br, ms, mr, ros, ror, rvs, rvr, rls, rlr, xs, xr, gs, gr, gls, glr,
+    din, ds_sem, das_sem, dar_sem,
 ):
     t = lax.axis_index("tm")
     b = lax.axis_index("band")
@@ -55,6 +56,8 @@
     slots = [k for k in range(K) if DISTANCES[k] < nt]
     chained = 2 in slots and 3 in slots
     near, far = 2, 3
+    step = DISTANCES[near]
+    detours = [k for k in (1, 0) if chained and nt % step == 0]
     log_chunks = (H * J) // CHUNK
 
     barrier = pltpu.get_barrier_semaphore()
@@ -88,8 +91,9 @@
 
     w_value_t[...] = w_value[...].astype(F32).T.astype(BF16)
     order_in = entry_order(0)
-    wl_t[...] = nt_dot(order_in, w_logit[...]).astype(BF16)
-    wl[...] = nt_dot(w_logit[...], order_in).astype(BF16)
+    ordered = dot(order_in, w_logit[...])
+    wl_t[...] = ordered.astype(BF16)
+    wl[...] = ordered.T.astype(BF16)
 
     def make_values(p, at):
         v = nt_dot(w_value_t[...], cells(feats, p)).astype(BF16)
@@ -112,7 +116,22 @@
     def sends_fwd(k):
         if chained and k == far:
             return (t >= DISTANCES[near]) & (t + DISTANCES[near] < nt)
-        return t + DISTANCES[k] < nt
+        ok = t + DISTANCES[k] < nt
+        return ok & (lax.rem(t + DISTANCES[k], step) >= DISTANCES[k]) if k in detours else ok
+
+    def relays(k):
+        return (t >= step) & (lax.rem(t, step) + DISTANCES[k] >= step)
+
+    def relay(k):
+        to = lax.rem(t + DISTANCES[k] - step + nt, nt)
+        return rc(main_of(near), main_of(k), ds_sem.at[k], fr.at[k], to, b)
+
+    def goes_around(k):
+        return (t >= DISTANCES[k]) & (lax.rem(t, step) < DISTANCES[k])
+
+    def around(k):
+        to = lax.rem(t + step - DISTANCES[k], nt)
+        return rc(cout.at[k], din.at[k], das_sem.at[k], dar_sem.at[k], to, b)
 
     order = [k for k in (2, 1, 0, 4) if k in slots]
     for k in order:
@@ -194,12 +213,14 @@
         return rc(cout.at[k], cin.at[k], bs.at[k], br.at[k], lax.rem(t - hop(k) + nt, nt), b)
 
     def sends_bwd(k):
-        return t >= DISTANCES[k]
+        ok = t >= DISTANCES[k]
+        return ok & (lax.rem(t, step) >= DISTANCES[k]) if k in detours else ok
 
     def gets_bwd(k):
         if chained and k == far:
             return (t >= DISTANCES[near]) & (t + DISTANCES[near] < nt)
-        return t + DISTANCES[k] < nt
+        ok = t + DISTANCES[k] < nt
+        return ok & (lax.rem(t + DISTANCES[k], step) >= DISTANCES[k]) if k in detours else ok
 
     def finish_contribution(k):
         for side in (0, 1):
@@ -219,6 +240,17 @@
 
                 loop(body)
 
+        if k == near:
+            for n in detours:
+                @pl.when(relays(n))
+                def _(n=n):
+                    around(n).wait_recv()
+
+                    def add(r):
+                        acc[k, r + 1] += din[n, r].astype(F32)
+
+                    loop(add)
+
         def body(r):
             cout[k, r] = acc[k, r + 1].astype(BF16)
 
@@ -227,6 +259,11 @@
         @pl.when(sends_bwd(k))
         def _():
             bwd(k).start()
+
+        if k in detours:
+            @pl.when(goes_around(k))
+            def _():
+                around(k).start()
 
     back_order = [k for k in (3, 1, 0, 2, 4) if k in slots]
     late = [near] if chained else []
@@ -288,12 +325,17 @@
         def _():
             fwd(far).start()
 
+    for k in detours:
+        @pl.when(relays(k))
+        def _(k=k):
+            relay(k).start()
+
+    for k in late:
+        finish_contribution(k)
     pairs(own_sample)
     for k in order:
         if not (chained and k == near):
             take(k)
-    for k in late:
-        finish_contribution(k)
     for k in order:
         sample(k)
     if far in slots:
@@ -490,6 +532,15 @@
         def _(k=k):
             bwd(k).wait_send()
 
+        if k in detours:
+            @pl.when(relays(k))
+            def _(k=k):
+                relay(k).wait_send()
+
+            @pl.when(goes_around(k))
+            def _(k=k):
+                around(k).wait_send()
+
         for side in (0, 1):
             @pl.when(has(side))
             def _(k=k, side=side):
@@ -504,7 +555,7 @@
     out_feats[...] = feats[...]
     out_wout[...] = sums[0].astype(F32)
     out_value[...] = sums[1].astype(F32).T
-    out_logit[...] = dot(entry_order(1), logs[...]).T
+    out_logit[...] = dot(entry_order(1), logs[...])
 
 
 def shards(nt, nb, feats, cotangent, w_value, w_logit, w_out, row_offsets, col_offsets, fractions, present):
@@ -548,6 +599,7 @@
         dma((nt,)), dma((nt,)), dma((nt,)), dma((nt,)), dma((nt,)), dma((nt,)),
         dma((nb,)), dma((nb,)),
         dma((nt,)), dma((nt,)), dma((nt,)), dma((nt,)),
+        v((2,) + grid, BF16), dma((2,)), dma((2,)), dma((2,)),
     ]
     grad_feats, sums, log_sums = pl.pallas_call(
         functools.partial(kernel, nt, nb, owners),
@@ -558,18 +610,19 @@
         compiler_params=pltpu.CompilerParams(
             collective_id=0, has_side_effects=True, vmem_limit_bytes=56 * 1024 * 1024
         ),
-    )(feats, cotangent, w_value, w_logit, w_out, row_offsets, col_offsets, fractions, present)
-    return pl.pallas_call(
+    )(feats, cotangent, w_value, w_logit.T, w_out, row_offsets, col_offsets, fractions, present)
+    outs = pl.pallas_call(
         unpack,
         out_shape=(
             jax.ShapeDtypeStruct(feats.shape, BF16),
             jax.ShapeDtypeStruct(square, F32),
-            jax.ShapeDtypeStruct(w_logit.shape, F32),
+            jax.ShapeDtypeStruct(logs, F32),
             jax.ShapeDtypeStruct(square, F32),
         ),
         in_specs=[vmem] * 3,
         out_specs=(vmem,) * 4,
     )(grad_feats, sums, log_sums)
+    return outs[0], outs[1], outs[2].T, outs[3]
 
 
 def solution(mesh):

time: 78 us -> 77.5 us (level)
  local copies, waits for them, and re-layouts: 3.07 us -> 0 us
  Pallas kernels: 74 us -> 76.6 us
    pallas_call x1, Pallas kernels: 71.8 us -> 74.5 us  [shards(): pl.pallas_call(functools.partial(kernel, nt, nb, owners), out_shape=tuple...]
    pallas_call x1 -> x0, local copies, waits for them, and re-layouts: 1.6 us -> none  [shards(): pl.pallas_call(unpack, out_shape=(jax.ShapeDtypeStruct(feats.shape, BF16)...]
    unnamed x1 -> x0, local copies, waits for them, and re-layouts: 1.47 us -> none
where the time goes in v3:
time: 77.5 us; the launch traced here: 77.3 us
  Pallas kernels  76.6 us (99%)
    pallas_call x1, Pallas kernels, shards(): pl.pallas_call(functools.partial(kernel, nt, nb, owners), out_shape=tuple...  74.5 us
    pallas_call x1, Pallas kernels, shards(): pl.pallas_call(unpack, out_shape=(jax.ShapeDtypeStruct(feats.shape, BF16)...  2.15 us

profile of v3, /device:TPU:0, one launch (start us, length us, event | category | flops | bytes accessed | tf_op | source)
XLA Modules:
  0.0 77.3 jit_solution(1867296563463644835)
XLA Ops:
  0.6 74.5 %shard_map.120 = (bf16[1,8,128,256]{3,2,1,0:T(8,128)(2,1)}, bf16[2,256,256]{2,1,0:T(8,128)(2,1)}, bf16[48,256]{1,0:T(8,128)(2,1)}) custom-call(bf16[1,8,128,256]{3,2,1,0:T(8,128)(2,1)} %feats.1, bf16[1,8,128,256]{3,2,1,0:T(8,128)(2,1)} %cot.1, bf16[256,256]{1,0:T(8,128)(2,1)} %w_value.1, bf16[48,256]{1,0:T(8,128)(2,1)} %bitcast.2, bf16[256,256]{1,0:T(8,128)(2,1)} %w_out.1, ...), custom_call_target="tpu_custom_call" | custom-call | tf_op jit(solution)/shard_map/pallas_call | solution.py:604
  75.1 2.1 %shard_map.121 = (bf16[1,8,128,256]{3,2,1,0:T(8,128)(2,1)}, f32[256,256]{1,0:T(8,128)}, f32[48,256]{1,0:T(8,128)}, f32[256,256]{1,0:T(8,128)}) custom-call(bf16[1,8,128,256]{3,2,1,0:T(8,128)(2,1)} %get-tuple-element.11.feats, bf16[2,256,256]{2,1,0:T(8,128)(2,1)} %get-tuple-element.12.sums, bf16[48,256]{1,0:T(8,128)(2,1)} %get-tuple-element.13.logs), custom_call_target="tpu_custom_call" | custom-call | tf_op jit(solution)/shard_map/pallas_call | solution.py:614
